TPU v7x, 512 devices: a whole 4x8x8 slice. The times are simulated.
512 devices in a mesh: dp: 32 (over x, y), tp: 16 (over z, core).
Axes of the slice: x: 4, y: 8, z: 8, core: 2. Of those that a mesh axis runs over, the one named last changes fastest.
Arguments:
- embeddings: bfloat16 [12288, 192, 256], P(('dp', 'tp')), may hold values from -6 to 6
- projection: bfloat16 [256, 16], replicated, may hold values from -0.375 to 0.375
- compress: bfloat16 [256, 4], replicated, may hold values from -0.375 to 0.375
- w_up: bfloat16 [4096, 4096], P(None, 'tp'), may hold values from -0.09375 to 0.09375
- w_down: bfloat16 [4096, 768], P('tp'), may hold values from -0.125 to 0.125
- output_norm_gain: float32 [1536], P('tp'), may hold values from 0.25 to 1.75
- out_grad: bfloat16 [12288, 1536], P('dp', 'tp'), may hold values from -6 to 6
Outputs:
- block_result: bfloat16 [12288, 1536], P('dp', 'tp')
- grad_down: float32 [4096, 768], P(('tp', 'dp'))
All inputs are finite; a program needn't handle non-finite values.
Results may differ from a plain program's by a relative error of at most 0.017.
Values may be sent and summed in bfloat16 or wider, within the bound.
No kernel may reach another device: no remote copies, remote signals or barrier semaphores. Data moves between devices by JAX's collectives and lax.ppermute only.
A program may use at most 64 MiB of HBM per device.

v0:
```python
import jax
import jax.numpy as jnp
from jax import lax
from jax.sharding import PartitionSpec as P


def split_up(x, dim, devices):
    before, after = (x.shape[:dim], x.shape[dim + 1 :])
    return jnp.moveaxis(x.reshape(*before, devices, -1, *after), dim, 0)


def summed_on_arrival(x, axis, dim):
    parts = split_up(x, dim, lax.axis_size(axis))
    arrived = lax.all_to_all(parts, axis, split_axis=0, concat_axis=0, tiled=True)
    return arrived.astype(jnp.float32).sum(axis=0)


def sent_to_all(x, axis):
    devices = lax.axis_size(axis)
    return lax.all_to_all(jnp.broadcast_to(x[None], (devices, *x.shape)), axis, 0, 0, tiled=True)


def gathered_once(x, axis):
    leaves = jax.tree.leaves(x)
    sequence = sorted(range(len(leaves)), key=lambda k: -leaves[k].size)
    width = (1, *leaves[sequence[0]].shape)[-1]
    lines = [
        jnp.pad(leaves[k].reshape(-1), (0, -leaves[k].size % width)).reshape(-1, width)
        for k in sequence
    ]
    both, at, found = (sent_to_all(jnp.concatenate(lines), axis), 0, {})
    for k, line in zip(sequence, lines):
        share = both[:, at : at + len(line)].reshape(len(both), -1)
        found[k] = share[:, : leaves[k].size].reshape(-1, *leaves[k].shape)
        at += len(line)
    numbers = iter(range(len(leaves)))
    return jax.tree.map(lambda _: found[next(numbers)], x)


def joined_by_halves(pieces, combine):
    while len(jax.tree.leaves(pieces)[0]) > 1:
        pieces = jax.vmap(combine)(
            *(jax.tree.map(lambda part: part[side::2], pieces) for side in (0, 1))
        )
    return jax.tree.map(lambda part: part[0], pieces)


def joined_all(x, axis, combine):
    pieces = gathered_once(x, axis)
    return joined_by_halves(pieces, combine)


def turned_gather(arrays, axis, dims):
    turned = [jnp.moveaxis(a, dim, 0) for a, dim in zip(arrays, dims)]
    both = jnp.concatenate([t.reshape(len(t), -1) for t in turned], axis=1)
    filled, at, done = (lax.all_gather(both, axis, axis=0, tiled=True), 0, [])
    for t, dim in zip(turned, dims):
        share = filled[:, at : at + t[0].size].reshape(-1, *t.shape[1:])
        done.append(jnp.moveaxis(share, 0, dim))
        at += t[0].size
    return tuple(done)


def chan_merge(left, right):
    count_a, mean_a, dev_a = left
    count_b, mean_b, dev_b = right
    total = count_a + count_b
    delta = mean_b - mean_a
    row_average = mean_a + delta * (count_b / total)
    dev = dev_a + dev_b + delta * delta * (count_a * count_b / total)
    return (total, row_average, dev)


def on_device(embeddings, projection, compress, w_up, w_down, output_norm_gain, out_grad):
    samples = embeddings.shape[0]
    pairs = jnp.einsum(
        "sef,fk->sek", embeddings, projection, preferred_element_type=jnp.float32
    ).astype(jnp.bfloat16)
    inter = jnp.einsum(
        "sek,sef->skf", pairs, embeddings, preferred_element_type=jnp.float32
    ).reshape(samples, -1)
    center = inter - jnp.mean(inter, axis=1, keepdims=True)
    spread = jnp.mean(center * center, axis=1, keepdims=True)
    normed = (center / jnp.sqrt(spread + 1e-05)).astype(jnp.bfloat16)
    lcb = jnp.einsum(
        "sef,fj->sje", embeddings, compress, preferred_element_type=jnp.float32
    ).reshape(samples, -1)
    hidden = jax.nn.gelu(
        jnp.dot(
            lax.all_gather(normed, "tp", axis=0, tiled=True),
            w_up,
            preferred_element_type=jnp.float32,
        ),
        approximate=True,
    ).astype(jnp.bfloat16)
    group_rows = hidden.shape[0]
    tp_count = lax.axis_size("tp")
    mlp = jnp.dot(hidden, w_down, preferred_element_type=jnp.float32)
    mlp_width = mlp.shape[1]
    full_width = mlp_width + lcb.shape[1]
    width = full_width // tp_count
    mlp_share = summed_on_arrival(mlp.astype(jnp.bfloat16), "tp", 1)
    lcb_share = lax.all_to_all(
        lcb.astype(jnp.bfloat16), "tp", split_axis=1, concat_axis=0, tiled=True
    ).astype(lcb.dtype)
    mixed_rows = jnp.concatenate([mlp_share, lcb_share], axis=1)
    own_mean = jnp.mean(mixed_rows, axis=1)
    own_dev = jnp.sum((mixed_rows - own_mean[:, None]) ** 2, axis=1)
    own_count = jnp.full((), width, jnp.float32)
    total, row_average, dev = joined_all((own_count, own_mean, own_dev), "tp", chan_merge)
    inverse_deviation = 1.0 / jnp.sqrt(dev[:, None] / total + 1e-05)
    centered_rows = (mixed_rows - row_average[:, None]) * inverse_deviation
    block_result = (centered_rows * output_norm_gain).astype(jnp.bfloat16)
    scaled_rows = out_grad.astype(jnp.float32) * output_norm_gain
    entire_scaled_rows, entire_normalized_rows = tuple(
        (
            part.astype(jnp.float32)
            for part in turned_gather(
                (scaled_rows.astype(jnp.bfloat16), centered_rows.astype(jnp.bfloat16)), "tp", (1, 1)
            )
        )
    )
    first_moment = jnp.mean(entire_scaled_rows, axis=1, keepdims=True)
    second_moment = jnp.mean(entire_scaled_rows * entire_normalized_rows, axis=1, keepdims=True)
    mixed_gradient = (
        (entire_scaled_rows - first_moment - entire_normalized_rows * second_moment)
        * inverse_deviation
    ).astype(jnp.bfloat16)
    group_mlp = mlp_width // tp_count
    mlp_grad = mixed_gradient.reshape(group_rows, tp_count, -1)[:, :, :group_mlp].reshape(
        group_rows, -1
    )
    grad_down = summed_on_arrival(
        jnp.einsum("rh,rc->hc", hidden, mlp_grad, preferred_element_type=jnp.float32).astype(
            jnp.bfloat16
        ),
        "dp",
        0,
    )
    return (block_result, grad_down)


def solution(mesh):
    return jax.shard_map(
        on_device,
        mesh=mesh,
        in_specs=(
            P(("dp", "tp"), None, None),
            P(),
            P(),
            P(None, "tp"),
            P("tp", None),
            P("tp"),
            P("dp", "tp"),
        ),
        out_specs=(P("dp", "tp"), P(("tp", "dp"), None)),
        check_vma=False,
    )
```

profile of v0, /device:TPU:8, one launch (start us, length us, event | category | flops | bytes accessed | tf_op | source)
XLA Modules:
  0.0 184.7 jit_solution(13328559922858504637)
XLA Ops:
  7.2 1.6 copy-done
  8.8 1.8 fusion.26
  10.7 0.4 multiply_reduce_fusion
  11.1 0.2 copy.26
  11.3 0.8 divide_convert_fusion
  12.1 0.7 fusion.6
  12.9 0.1 convert_element_type.74
  13.0 0.8 reshape.145
  13.8 10.4 %all-to-all-start.1 = ((bf16[16,2,576]{2,1,0:T(2,128)(2,1)}), bf16[16,2,576]{2,1,0:T(2,128)(2,1)S(1)}, u32[]{:S(2)}, u32[]{:S(2)}) async-start(bf16[16,2,576]{2,1,0:T(2,128)(2,1)} %reshape.145), calls=%async_computation.1 | async-start | bytes 81920 | tf_op jit(solution)/shard_map/all_to_all | solution.py:103
  24.2 37.1 %all-gather.3.cloned.1.call-done = bf16[384,4096]{1,0:T(8,128)(2,1)} async-done(((bf16[24,4096]{1,0:T(8,128)(2,1)}), bf16[384,4096]{1,0:T(8,128)(2,1)}) %all-gather.3.cloned.1.call-update) | async-done | bytes 3145744 | tf_op jit(solution)/shard_map/all_gather | solution.py:90
  61.3 3.6 %fusion.29 = f32[384,256]{1,0:T(8,128)S(1)} fusion(bf16[384,4096]{1,0:T(8,128)(2,1)} %all-gather.3.cloned.1.call-done, bf16[4096,256]{1,0:T(8,128)(2,1)} %param.10), kind=kOutput, calls=%fused_computation.71 | convolution fusion | flops 805306368 | bytes 5636096 | tf_op jit(solution)/shard_map/dot_general | solution.py:89
  64.9 0.7 copy-done.7
  65.7 0.4 convolution_convert_fusion
  66.1 1.0 copy.19
  67.1 4.3 %all-to-all-start = ((bf16[16,384,48]{1,2,0:T(8,128)(2,1)}), bf16[16,384,48]{1,2,0:T(8,128)(2,1)S(1)}, u32[]{:S(2)}, u32[]{:S(2)}) async-start(bf16[16,384,48]{1,2,0:T(8,128)(2,1)} %bitcast.2), calls=%async_computation | async-start | bytes 1179648 | tf_op jit(solution)/shard_map/all_to_all | solution.py:14
  71.5 0.1 reshape.146
  71.6 0.1 convert_reduce_fusion.4
  72.1 16.6 %all-to-all-done = bf16[16,384,48]{1,2,0:T(8,128)(2,1)S(1)} async-done(((bf16[16,384,48]{1,2,0:T(8,128)(2,1)}), bf16[16,384,48]{1,2,0:T(8,128)(2,1)S(1)}, u32[]{:S(2)}, u32[]{:S(2)}) %all-to-all-start) | async-done | bytes 589856 | tf_op jit(solution)/shard_map/all_to_all | solution.py:14
  88.7 0.2 convert_reduce_fusion.1
  89.0 12.5 %all_to_all.25 = f32[16,3,384]{2,1,0:T(4,128)S(1)} all-to-all(f32[16,3,384]{2,1,0:T(4,128)S(1)} %broadcast_in_dim.2), channel_id=1, replica_groups=mesh['dp'=32,'tp'=16] {'tp'}, dimensions={0} | all-to-all | bytes 147456 | tf_op jit(solution)/shard_map/all_to_all | solution.py:20
  101.7 0.1 slice_reduce_fusion
  102.4 0.6 fusion.25
  106.8 0.7 fusion.16
  107.5 0.7 pad_maximum_fusion.1
  108.2 40.1 %all-gather.5.cloned.1.call-done = bf16[1536,768]{1,0:T(8,128)(2,1)} async-done(((bf16[96,768]{1,0:T(8,128)(2,1)}), bf16[1536,768]{1,0:T(8,128)(2,1)}) %all-gather.5.cloned.1.call-update) | async-done | bytes 2359312 | tf_op jit(solution)/shard_map/all_gather | solution.py:56
  148.3 2.2 %convert_reduce_fusion = (f32[384]{0:T(512)S(1)}, f32[384]{0:T(512)S(1)}) fusion(bf16[1536,768]{1,0:T(8,128)(2,1)} %all-gather.5.cloned.1.call-done), kind=kLoop, calls=%fused_computation.2 | loop fusion | flops 2948352 | bytes 2362368 | tf_op jit(solution)/shard_map/reduce_sum | solution.py:123
  150.6 0.1 copy-done.1
  150.7 0.5 fusion.2
  151.3 0.4 copy-done.8
  151.7 0.5 fusion.4
  152.2 25.1 %all_to_all.26 = bf16[32,8,768]{2,1,0:T(8,128)(2,1)S(1)} all-to-all(bf16[32,8,768]{2,1,0:T(8,128)(2,1)S(1)} %fusion.4), channel_id=1, replica_groups=mesh['dp'=32,'tp'=16] {'dp'}, dimensions={0} | all-to-all | bytes 786432 | tf_op jit(solution)/shard_map/all_to_all | solution.py:14
  177.2 0.7 convert_reduce_fusion.3
  (66 shorter events, 1.8 us)
Async XLA Ops:
  7.2 1.7 copy-start
  7.2 5.0 %copy-start.3 = (bf16[256,4]{0,1:T(4,128)(2,1)S(1)}, bf16[256,4]{0,1:T(4,128)(2,1)}, u32[]{:S(2)}) copy-start(bf16[256,4]{0,1:T(4,128)(2,1)} %param.9) | copy-start | bytes 6148
  7.2 54.2 %all-gather.3.cloned.1.call-start = ((), (), s32[]{:S(2)}) async-start(), calls=%async_computation.4 | async-start | bytes 3342336 | tf_op jit(solution)/shard_map/all_gather | solution.py:90
  13.8 53.3 %all-to-all-start.1 = ((bf16[16,2,576]{2,1,0:T(2,128)(2,1)}), bf16[16,2,576]{2,1,0:T(2,128)(2,1)S(1)}, u32[]{:S(2)}, u32[]{:S(2)}) async-start(bf16[16,2,576]{2,1,0:T(2,128)(2,1)} %reshape.145), calls=%async_computation.1 | async-start | bytes 81920 | tf_op jit(solution)/shard_map/all_to_all | solution.py:103
  61.3 4.3 %copy-start.6 = (bf16[256,768]{1,0:T(8,128)(2,1)S(1)}, bf16[256,768]{1,0:T(8,128)(2,1)}, u32[]{:S(2)}) copy-start(bf16[256,768]{1,0:T(8,128)(2,1)} %param.11) | copy-start | bytes 1179652
  64.9 0.7 copy-start.7
  66.0 22.9 %copy-start.4 = (f32[1,384]{1,0:T(1,128)S(1)}, f32[1,384]{1,0:T(1,128)}, u32[]{:S(2)}) copy-start(f32[1,384]{1,0:T(1,128)} %constant.29.clone.1) | copy-start | bytes 4612
  66.1 40.7 %copy-start.2 = (bf16[384,96]{0,1:T(8,128)(2,1)S(1)}, bf16[384,96]{0,1:T(8,128)(2,1)}, u32[]{:S(2)}) copy-start(bf16[384,96]{0,1:T(8,128)(2,1)} %param.13) | copy-start | bytes 221188
  66.1 40.7 %copy-start.5 = (f32[96]{0:T(128)S(1)}, f32[96]{0:T(128)}, u32[]{:S(2)}) copy-start(f32[96]{0:T(128)} %param.12) | copy-start | bytes 1156
  67.1 21.5 %all-to-all-start = ((bf16[16,384,48]{1,2,0:T(8,128)(2,1)}), bf16[16,384,48]{1,2,0:T(8,128)(2,1)S(1)}, u32[]{:S(2)}, u32[]{:S(2)}) async-start(bf16[16,384,48]{1,2,0:T(8,128)(2,1)} %bitcast.2), calls=%async_computation | async-start | bytes 1179648 | tf_op jit(solution)/shard_map/all_to_all | solution.py:14
  71.4 76.9 %all-gather.5.cloned.1.call-start = ((), (), s32[]{:S(2)}) async-start(), calls=%async_computation.5 | async-start | bytes 2506752 | tf_op jit(solution)/shard_map/all_gather | solution.py:56
  148.3 2.4 %copy-start.1 = (bf16[1536,768]{1,0:T(8,128)(2,1)S(1)}, bf16[1536,768]{1,0:T(8,128)(2,1)}, u32[]{:S(2)}) copy-start(bf16[1536,768]{1,0:T(8,128)(2,1)} %all-gather.5.cloned.1.call-done) | copy-start | bytes 7077892
  150.7 1.0 copy-start.8
Sparse Core Ops, SparseCore 0:
  12.3 49.0 all-gather.2
  108.3 39.9 all-gather.4
where the time goes:
time: 185 us
  waiting for transfers between devices  93.8 us (51%)
  blocking collectives  37.6 us (20%)
  between operations  17.6 us (10%)
  starting transfers between devices  14.8 us (8%)
  local copies, waits for them, and re-layouts  7.2 us (4%)
  matrix products  6.93 us (4%)
  other arithmetic  6.77 us (4%)
    all_gather x1, waiting for transfers between devices, turned_gather(): filled, at, done = (lax.all_gather(both, axis, axis=0, tiled=True), 0, [])  40.1 us
    all_gather x1, waiting for transfers between devices, on_device(): lax.all_gather(normed, 'tp', axis=0, tiled=True)  37.1 us
    all_to_all x1, blocking collectives, summed_on_arrival(): lax.all_to_all(parts, axis, split_axis=0, concat_axis=0, tiled=True)  25.1 us
    all_to_all x1, waiting for transfers between devices, summed_on_arrival(): lax.all_to_all(parts, axis, split_axis=0, concat_axis=0, tiled=True)  16.6 us
    all_to_all x1, blocking collectives, sent_to_all(): lax.all_to_all(jnp.broadcast_to(x[None], (devices, *x.shape)), axis, 0, 0...  12.5 us
    all_to_all x1, starting transfers between devices, on_device(): lax.all_to_all(lcb.astype(jnp.bfloat16), 'tp', split_axis=1, concat_axis=...  10.4 us
    all_to_all x1, starting transfers between devices, summed_on_arrival(): lax.all_to_all(parts, axis, split_axis=0, concat_axis=0, tiled=True)  4.3 us
    unnamed x22, local copies, waits for them, and re-layouts  4.06 us
  transfers between devices with their start and end apart: 4, of which 3 were waited for; matrix products, arithmetic and copies ran while one was open for 4% of the time, Pallas kernels for 0%

commit v1 on v0

--- a/solution.py
+++ b/solution.py
@@ -2,6 +2,11 @@
 import jax.numpy as jnp
 from jax import lax
 from jax.sharding import PartitionSpec as P
+
+
+def all_by_exchange(array, axis, along):
+    sent = jnp.stack([array] * lax.axis_size(axis))
+    return jnp.concatenate(lax.all_to_all(sent, axis, 0, 0), axis=along)
 
 
 def split_up(x, dim, devices):
@@ -53,7 +58,7 @@
 def turned_gather(arrays, axis, dims):
     turned = [jnp.moveaxis(a, dim, 0) for a, dim in zip(arrays, dims)]
     both = jnp.concatenate([t.reshape(len(t), -1) for t in turned], axis=1)
-    filled, at, done = (lax.all_gather(both, axis, axis=0, tiled=True), 0, [])
+    filled, at, done = (all_by_exchange(both, axis, 0), 0, [])
     for t, dim in zip(turned, dims):
         share = filled[:, at : at + t[0].size].reshape(-1, *t.shape[1:])
         done.append(jnp.moveaxis(share, 0, dim))

time: 185 us -> 202 us (1.092)
  blocking collectives: 37.6 us -> 96.7 us
  waiting for transfers between devices: 93.8 us -> 53.7 us
  other arithmetic: 6.77 us -> 4.33 us
    all_to_all x0 -> x1, blocking collectives: none -> 58.7 us  [all_by_exchange(): return jnp.concatenate(lax.all_to_all(sent, axis, 0, 0), axis=along)]
    all_gather x1 -> x0, waiting for transfers between devices: 40.1 us -> none  [turned_gather(): filled, at, done = (lax.all_gather(both, axis, axis=0, tiled=True), 0, [])]
    unnamed x22 -> x20, local copies, waits for them, and re-layouts: 4.06 us -> 3.93 us
  transfers between devices with their start and end apart: 4 -> 3, of which waited for: 3 -> 2; matrix products, arithmetic and copies ran while one was open for 4% -> 4% of each run, Pallas kernels for 0% -> 0%
where the time goes in v1:
time: 202 us; the launch traced here: 201 us
  blocking collectives  96.7 us (48%)
  waiting for transfers between devices  53.7 us (27%)
  between operations  17.6 us (9%)
  starting transfers between devices  14.8 us (7%)
  local copies, waits for them, and re-layouts  7.31 us (4%)
  matrix products  6.93 us (3%)
  other arithmetic  4.33 us (2%)
    all_to_all x1, blocking collectives, all_by_exchange(): return jnp.concatenate(lax.all_to_all(sent, axis, 0, 0), axis=along)  58.7 us
    all_gather x1, waiting for transfers between devices, on_device(): lax.all_gather(normed, 'tp', axis=0, tiled=True)  37.1 us
    all_to_all x1, blocking collectives, summed_on_arrival(): lax.all_to_all(parts, axis, split_axis=0, concat_axis=0, tiled=True)  25.5 us
    all_to_all x1, waiting for transfers between devices, summed_on_arrival(): lax.all_to_all(parts, axis, split_axis=0, concat_axis=0, tiled=True)  16.6 us
    all_to_all x1, blocking collectives, sent_to_all(): lax.all_to_all(jnp.broadcast_to(x[None], (devices, *x.shape)), axis, 0, 0...  12.5 us
    all_to_all x1, starting transfers between devices, on_device(): lax.all_to_all(lcb.astype(jnp.bfloat16), 'tp', split_axis=1, concat_axis=...  10.4 us
    all_to_all x1, starting transfers between devices, summed_on_arrival(): lax.all_to_all(parts, axis, split_axis=0, concat_axis=0, tiled=True)  4.3 us
  transfers between devices with their start and end apart: 3, of which 2 were waited for; matrix products, arithmetic and copies ran while one was open for 4% of the time, Pallas kernels for 0%

profile of v1, /device:TPU:8, one launch (start us, length us, event | category | flops | bytes accessed | tf_op | source)
XLA Modules:
  0.0 201.4 jit_solution(371226531162347347)
XLA Ops:
  7.2 1.6 copy-done
  8.8 1.8 fusion.26
  10.7 0.4 multiply_reduce_fusion
  11.1 0.2 copy.31
  11.3 0.8 divide_convert_fusion
  12.1 0.7 fusion.6
  12.9 0.1 convert_element_type.74
  13.0 0.8 reshape.151
  13.8 10.4 %all-to-all-start.1 = ((bf16[16,2,576]{2,1,0:T(2,128)(2,1)}), bf16[16,2,576]{2,1,0:T(2,128)(2,1)S(1)}, u32[]{:S(2)}, u32[]{:S(2)}) async-start(bf16[16,2,576]{2,1,0:T(2,128)(2,1)} %reshape.151), calls=%async_computation.1 | async-start | bytes 81920 | tf_op jit(solution)/shard_map/all_to_all | solution.py:108
  24.2 37.1 %all-gather.2.cloned.1.call-done = bf16[384,4096]{1,0:T(8,128)(2,1)} async-done(((bf16[24,4096]{1,0:T(8,128)(2,1)}), bf16[384,4096]{1,0:T(8,128)(2,1)}) %all-gather.2.cloned.1.call-update) | async-done | bytes 3145744 | tf_op jit(solution)/shard_map/all_gather | solution.py:95
  61.3 3.6 %fusion.29 = f32[384,256]{1,0:T(8,128)S(1)} fusion(bf16[384,4096]{1,0:T(8,128)(2,1)} %all-gather.2.cloned.1.call-done, bf16[4096,256]{1,0:T(8,128)(2,1)} %param.10), kind=kOutput, calls=%fused_computation.71 | convolution fusion | flops 805306368 | bytes 5636096 | tf_op jit(solution)/shard_map/dot_general | solution.py:94
  64.9 0.7 copy-done.6
  65.7 0.4 convolution_convert_fusion
  66.1 1.0 copy.24
  67.1 4.3 %all-to-all-start = ((bf16[16,384,48]{1,2,0:T(8,128)(2,1)}), bf16[16,384,48]{1,2,0:T(8,128)(2,1)S(1)}, u32[]{:S(2)}, u32[]{:S(2)}) async-start(bf16[16,384,48]{1,2,0:T(8,128)(2,1)} %bitcast.2), calls=%async_computation | async-start | bytes 1179648 | tf_op jit(solution)/shard_map/all_to_all | solution.py:19
  71.4 0.1 reshape.152
  71.6 0.1 convert_reduce_fusion.4
  71.9 0.1 copy.26
  72.0 16.6 %all-to-all-done = bf16[16,384,48]{1,2,0:T(8,128)(2,1)S(1)} async-done(((bf16[16,384,48]{1,2,0:T(8,128)(2,1)}), bf16[16,384,48]{1,2,0:T(8,128)(2,1)S(1)}, u32[]{:S(2)}, u32[]{:S(2)}) %all-to-all-start) | async-done | bytes 589856 | tf_op jit(solution)/shard_map/all_to_all | solution.py:19
  88.7 0.2 convert_reduce_fusion.1
  89.0 12.5 %all_to_all.30 = f32[16,3,384]{2,1,0:T(4,128)S(1)} all-to-all(f32[16,3,384]{2,1,0:T(4,128)S(1)} %broadcast_in_dim.2), channel_id=1, replica_groups=mesh['dp'=32,'tp'=16] {'tp'}, dimensions={0} | all-to-all | bytes 147456 | tf_op jit(solution)/shard_map/all_to_all | solution.py:25
  101.7 0.1 slice_reduce_fusion
  102.4 0.6 fusion.25
  106.8 0.7 fusion.16
  107.5 0.2 stack.2
  107.8 58.7 %all_to_all.31 = bf16[16,96,768]{2,1,0:T(8,128)(2,1)S(1)} all-to-all(bf16[16,96,768]{2,1,0:T(8,128)(2,1)S(1)} %stack.2), channel_id=1, replica_groups=mesh['dp'=32,'tp'=16] {'tp'}, dimensions={0} | all-to-all | bytes 4718592 | tf_op jit(solution)/shard_map/all_to_all | solution.py:9
  166.5 0.5 convert_reduce_fusion
  166.9 0.5 fusion.2
  167.5 0.4 copy-done.7
  167.9 0.5 fusion.4
  168.4 25.5 %all_to_all.32 = bf16[32,8,768]{2,1,0:T(8,128)(2,1)S(1)} all-to-all(bf16[32,8,768]{2,1,0:T(8,128)(2,1)S(1)} %fusion.4), channel_id=1, replica_groups=mesh['dp'=32,'tp'=16] {'dp'}, dimensions={0} | all-to-all | bytes 786432 | tf_op jit(solution)/shard_map/all_to_all | solution.py:19
  193.9 0.7 convert_reduce_fusion.3
  (63 shorter events, 1.7 us)
Async XLA Ops:
  7.2 1.7 copy-start
  7.2 5.0 %copy-start.2 = (bf16[256,4]{0,1:T(4,128)(2,1)S(1)}, bf16[256,4]{0,1:T(4,128)(2,1)}, u32[]{:S(2)}) copy-start(bf16[256,4]{0,1:T(4,128)(2,1)} %param.9) | copy-start | bytes 6148
  7.2 54.2 %all-gather.2.cloned.1.call-start = ((), (), s32[]{:S(2)}) async-start(), calls=%async_computation.5 | async-start | bytes 3342336 | tf_op jit(solution)/shard_map/all_gather | solution.py:95
  13.8 53.3 %all-to-all-start.1 = ((bf16[16,2,576]{2,1,0:T(2,128)(2,1)}), bf16[16,2,576]{2,1,0:T(2,128)(2,1)S(1)}, u32[]{:S(2)}, u32[]{:S(2)}) async-start(bf16[16,2,576]{2,1,0:T(2,128)(2,1)} %reshape.151), calls=%async_computation.1 | async-start | bytes 81920 | tf_op jit(solution)/shard_map/all_to_all | solution.py:108
  61.3 4.3 %copy-start.5 = (bf16[256,768]{1,0:T(8,128)(2,1)S(1)}, bf16[256,768]{1,0:T(8,128)(2,1)}, u32[]{:S(2)}) copy-start(bf16[256,768]{1,0:T(8,128)(2,1)} %param.11) | copy-start | bytes 1179652
  64.9 0.7 copy-start.6
  66.0 22.9 %copy-start.3 = (f32[1,384]{1,0:T(1,128)S(1)}, f32[1,384]{1,0:T(1,128)}, u32[]{:S(2)}) copy-start(f32[1,384]{1,0:T(1,128)} %constant.29.clone.1) | copy-start | bytes 4612
  66.1 40.7 %copy-start.1 = (bf16[384,96]{0,1:T(8,128)(2,1)S(1)}, bf16[384,96]{0,1:T(8,128)(2,1)}, u32[]{:S(2)}) copy-start(bf16[384,96]{0,1:T(8,128)(2,1)} %param.13) | copy-start | bytes 221188
  66.1 40.7 %copy-start.4 = (f32[96]{0:T(128)S(1)}, f32[96]{0:T(128)}, u32[]{:S(2)}) copy-start(f32[96]{0:T(128)} %param.12) | copy-start | bytes 1156
  67.1 21.5 %all-to-all-start = ((bf16[16,384,48]{1,2,0:T(8,128)(2,1)}), bf16[16,384,48]{1,2,0:T(8,128)(2,1)S(1)}, u32[]{:S(2)}, u32[]{:S(2)}) async-start(bf16[16,384,48]{1,2,0:T(8,128)(2,1)} %bitcast.2), calls=%async_computation | async-start | bytes 1179648 | tf_op jit(solution)/shard_map/all_to_all | solution.py:19
  166.9 1.0 copy-start.7
Sparse Core Ops, SparseCore 0:
  12.3 49.0 all-gather.1
